TPU v7x, 512 devices: a whole 4x4x16 slice. The times are simulated.
512 devices in a mesh: ctx: 16 (over x, y), exp: 32 (over z, core).
Axes of the slice: x: 4, y: 4, z: 16, core: 2. Of those that a mesh axis runs over, the one named last changes fastest.
Arguments:
- resid: bfloat16 [2048, 3072], P('ctx', 'exp'), may hold values from -37 to 37
- queries: bfloat16 [2048, 4096], P('ctx', 'exp'), may hold values from -6 to 6
- keys: bfloat16 [2048, 4096], P('ctx', 'exp'), may hold values from -0.01171875 to 0.01171875
- values: bfloat16 [2048, 4096], P('ctx', 'exp'), may hold values from -6 to 6
- log_decay: float32 [32, 2048], P('exp', 'ctx'), may hold values from -1.5 to 0
- w_out: bfloat16 [4096, 3072], P('exp'), may hold values from -0.1875 to 0.1875
- w_up: bfloat16 [32, 3072, 6144], P('exp', None, 'ctx'), may hold values from -0.07307089 to 0.07307089
- w_down: bfloat16 [32, 6144, 3072], P('exp', 'ctx'), may hold values from -0.076546554 to 0.076546554
- expert_ids: int32 [2048, 2], P('ctx'), may hold values from 0 to 31, all different within a row; in each aligned block of 128 rows (0 to 127, 128 to 255, ...) at most 16 rows name the same one
- route_weights: float32 [2048, 2], P('ctx'), may hold values from 0.3 to 1.5
- cotangent: bfloat16 [2048, 3072], P('ctx', 'exp'), may hold values from -6 to 6
Outputs:
- layer_out: bfloat16 [2048, 3072], P('ctx', 'exp')
- resid_grad: bfloat16 [2048, 3072], P('ctx', 'exp')
- q_grad: bfloat16 [2048, 4096], P('ctx', 'exp')
- k_grad: bfloat16 [2048, 4096], P('ctx', 'exp')
- v_grad: bfloat16 [2048, 4096], P('ctx', 'exp')
Inputs may be any that keep to these rules, and one draw needn't show every extreme that they name: `expert_ids`: in each aligned block of 128 rows (the positions of one block) no expert is named by more than 16 rows; the two ids of a row differ.
All inputs are finite; a program needn't handle non-finite values.
Results may differ from a plain program's by a relative error of at most 0.02.
Values may be sent and summed in bfloat16 or wider, within the bound.
No kernel may reach another device: no remote copies, remote signals or barrier semaphores. Data moves between devices by JAX's collectives and lax.ppermute only.
A program may use at most 64 MiB of HBM per device.

v0:
```python
import jax
import jax.numpy as jnp
from jax import lax
from jax.sharding import PartitionSpec as P

highest_score = lax.Precision.HIGHEST


def prefix(shard, axis, join, neutral, backward):
    count = lax.axis_size(axis)
    place = lax.axis_index(axis)
    ahead = count - 1 - place if backward else place
    gathered = jax.tree.map(
        lambda a, kind: lax.all_gather(a.astype(kind), axis), shard, (jnp.bfloat16, jnp.bfloat16)
    )
    state = jax.tree.map(lambda a, e: jnp.zeros_like(a) + jnp.asarray(e, a.dtype), shard, neutral)

    def one(hop, state):
        source = count - 1 - hop if backward else hop
        return join(
            state,
            jax.tree.map(
                lambda a, own: lax.dynamic_index_in_dim(a, source, 0, False).astype(own.dtype),
                gathered,
                shard,
            ),
        )

    return lax.fori_loop(0, ahead, one, state)


def block_decays(decay_rows):
    cum = jnp.cumsum(decay_rows, axis=-1)
    last = cum[:, -1]
    token_offset = jnp.arange(decay_rows.shape[-1])
    causal = token_offset[:, None] >= token_offset[None, :]
    gaps = jnp.where(causal[None], cum[:, :, None] - cum[:, None, :], -jnp.inf)
    return (cum, last, jnp.exp(gaps))


def silu_grad(upper):
    sigma = jax.nn.sigmoid(upper)
    return sigma * (1.0 + upper * (1.0 - sigma))


def split_heads(matrix, head_count):
    tokens_here = matrix.shape[0]
    return matrix.astype(jnp.float32).reshape(tokens_here, head_count, -1).transpose(1, 0, 2)


def join_heads(blocks):
    return blocks.transpose(1, 0, 2).reshape(blocks.shape[1], -1).astype(jnp.bfloat16)


def local(
    resid,
    queries,
    keys,
    values,
    log_decay,
    w_out,
    w_up,
    w_down,
    expert_ids,
    route_weights,
    cotangent,
):
    head_count = log_decay.shape[0]
    tokens_here = queries.shape[0]
    query_heads = split_heads(queries, head_count)
    head_keys = split_heads(keys, head_count)
    head_values = split_heads(values, head_count)
    cum, last, decay_matrix = block_decays(log_decay)
    keep_mask = jnp.exp(last[:, None] - cum)[..., None]
    router_scores = (
        jnp.einsum("htd,hid->hti", query_heads, head_keys, precision=highest_score) * decay_matrix
    )
    local_state = jnp.einsum(
        "hid,hie->hde", head_keys * keep_mask, head_values, precision=highest_score
    )

    def link(early, later):
        return (early[0] + later[0], jnp.exp(later[0])[:, None, None] * early[1] + later[1])

    blank = (jnp.zeros_like(last), jnp.zeros_like(local_state))
    _, incoming = prefix((last, local_state), "ctx", link, blank, False)
    inner = jnp.einsum("hti,hid->htd", router_scores, head_values, precision=highest_score)
    outer = jnp.exp(cum)[..., None] * jnp.einsum(
        "htd,hde->hte", query_heads, incoming, precision=highest_score
    )
    attn_heads = join_heads(inner + outer)
    width = w_out.shape[1]
    share = width // lax.axis_size("exp")
    columns = w_out
    attn = (
        lax.psum_scatter(
            lax.dot_general(
                columns, attn_heads, (((0,), (1,)), ((), ())), preferred_element_type=jnp.float32
            ).astype(jnp.bfloat16),
            "exp",
            scatter_dimension=0,
            tiled=True,
        )
        .astype(jnp.float32)
        .T.astype(jnp.bfloat16)
    )
    residual = (resid.astype(jnp.float32) + attn.astype(jnp.float32)).astype(jnp.bfloat16)
    residual_f = residual.astype(jnp.float32)
    square_sum = lax.psum(jnp.sum(residual_f * residual_f, axis=1), "exp")
    rstd = lax.rsqrt(square_sum / width + 1e-06)
    normed = (residual_f * rstd[:, None]).astype(jnp.bfloat16)
    expert_count = w_up.shape[0] * lax.axis_size("exp")
    capacity = 4 * tokens_here // expert_count
    onehot = (expert_ids[:, :, None] == jnp.arange(expert_count)[None, None, :]).astype(jnp.int32)
    flat = onehot.reshape(tokens_here * 2, expert_count)
    before = jnp.cumsum(flat, axis=0) - flat
    slots = jnp.sum(before * flat, axis=1).reshape(tokens_here, 2)
    position = expert_ids * capacity + slots
    place = position[:, :, None] == jnp.arange(expert_count * capacity)[None, None, :]
    picks = place.astype(jnp.bfloat16)
    placed = jnp.sum(place.astype(jnp.int32), axis=1).astype(jnp.bfloat16)
    sent_rows = lax.dot_general(
        placed, normed, (((0,), (0,)), ((), ())), preferred_element_type=jnp.float32
    )
    sent_rows = sent_rows.astype(jnp.bfloat16).reshape(expert_count, capacity, share)
    expert_in = lax.all_to_all(sent_rows, "exp", split_axis=0, concat_axis=2, tiled=True)
    all_rows = lax.all_gather(expert_in, "ctx", axis=1, tiled=True)
    upper = jnp.einsum("erd,edf->erf", all_rows, w_up, preferred_element_type=jnp.float32)
    act = jax.nn.silu(upper).astype(jnp.bfloat16)
    partial_out = jnp.einsum("erf,efd->erd", act, w_down, preferred_element_type=jnp.float32)
    expert_out = lax.psum_scatter(
        partial_out.astype(jnp.bfloat16), "ctx", scatter_dimension=1, tiled=True
    )
    returned = lax.all_to_all(expert_out, "exp", split_axis=2, concat_axis=0, tiled=True).reshape(
        expert_count * capacity, share
    )
    routed = jnp.einsum("tks,sd->tkd", picks, returned, preferred_element_type=jnp.float32)
    layer_out = (residual_f + jnp.sum(route_weights[:, :, None] * routed, axis=1)).astype(
        jnp.bfloat16
    )
    cot_f = cotangent.astype(jnp.float32)
    slot_weight = jnp.einsum(
        "tks,tk->s", place.astype(jnp.float32), route_weights, precision=highest_score
    )
    grad_rows_local = lax.dot_general(
        placed, cotangent, (((0,), (0,)), ((), ())), preferred_element_type=jnp.float32
    )
    grad_send = (
        (grad_rows_local * slot_weight[:, None])
        .astype(jnp.bfloat16)
        .reshape(expert_count, capacity, share)
    )
    grad_in = lax.all_to_all(grad_send, "exp", split_axis=0, concat_axis=2, tiled=True)
    grad_all = lax.all_gather(grad_in, "ctx", axis=1, tiled=True)
    grad_act = jnp.einsum("erd,efd->erf", grad_all, w_down, preferred_element_type=jnp.float32)
    grad_up = (grad_act * silu_grad(upper)).astype(jnp.bfloat16)
    partial_grad = jnp.einsum("erf,edf->erd", grad_up, w_up, preferred_element_type=jnp.float32)
    grad_expert = lax.psum_scatter(
        partial_grad.astype(jnp.bfloat16), "ctx", scatter_dimension=1, tiled=True
    )
    grad_back = lax.all_to_all(grad_expert, "exp", split_axis=2, concat_axis=0, tiled=True).reshape(
        expert_count * capacity, share
    )
    grad_normed = jnp.dot(placed, grad_back, preferred_element_type=jnp.float32)
    inner_dot = lax.psum(jnp.sum(grad_normed * residual_f, axis=1), "exp")
    grad_resid = (
        rstd[:, None] * grad_normed - residual_f * (rstd * rstd * rstd * inner_dot / width)[:, None]
    )
    resid_grad = (cot_f + grad_resid).astype(jnp.bfloat16)
    columns = w_out
    grad_flat = lax.dot_general(
        lax.all_gather(resid_grad, "exp", axis=1, tiled=True),
        columns,
        (((1,), (1,)), ((), ())),
        preferred_element_type=jnp.float32,
    )
    head_gradient = split_heads(grad_flat, head_count)
    local_grad = jnp.einsum(
        "hta,htb->hab",
        query_heads * jnp.exp(cum)[..., None],
        head_gradient,
        precision=highest_score,
    )

    def back_link(early, later):
        return (early[0] + later[0], later[1] + jnp.exp(later[0])[:, None, None] * early[1])

    blank_grad = (jnp.zeros_like(last), jnp.zeros_like(local_grad))
    _, carried_state = prefix((last, local_grad), "ctx", back_link, blank_grad, True)
    score_gradient = (
        jnp.einsum("coy,cwy->cow", head_gradient, head_values, precision=highest_score)
        * decay_matrix
    )
    query_grad = jnp.einsum("hti,hia->hta", score_gradient, head_keys, precision=highest_score)
    query_grad = query_grad + jnp.exp(cum)[..., None] * jnp.einsum(
        "htb,hab->hta", head_gradient, incoming, precision=highest_score
    )
    key_gradient = jnp.einsum("hti,hta->hia", score_gradient, query_heads, precision=highest_score)
    key_gradient = key_gradient + keep_mask * jnp.einsum(
        "qsv,qnv->qsn", head_values, carried_state, precision=highest_score
    )
    value_gradient = jnp.einsum(
        "nyw,nyx->nwx", router_scores, head_gradient, precision=highest_score
    )
    value_gradient = value_gradient + keep_mask * jnp.einsum(
        "sfc,scl->sfl", head_keys, carried_state, precision=highest_score
    )
    return (
        layer_out,
        resid_grad,
        join_heads(query_grad),
        join_heads(key_gradient),
        join_heads(value_gradient),
    )


def solution(mesh):
    return jax.shard_map(
        local,
        mesh=mesh,
        in_specs=(
            P("ctx", "exp"),
            P("ctx", "exp"),
            P("ctx", "exp"),
            P("ctx", "exp"),
            P("exp", "ctx"),
            P("exp", None),
            P("exp", None, "ctx"),
            P("exp", "ctx", None),
            P("ctx", None),
            P("ctx", None),
            P("ctx", "exp"),
        ),
        out_specs=(
            P("ctx", "exp"),
            P("ctx", "exp"),
            P("ctx", "exp"),
            P("ctx", "exp"),
            P("ctx", "exp"),
        ),
        check_vma=False,
    )
```

profile of v0, /device:TPU:32, one launch (start us, length us, event | category | flops | bytes accessed | tf_op | source)
XLA Modules:
  0.0 780.2 jit_solution(4295536002061562439)
XLA Ops:
  7.3 1.1 reduce_window_sum.26
  10.3 1.3 dynamic-slice
  11.6 1.1 convolution_convert_fusion.5
  12.7 0.8 dynamic-update-slice
  13.5 26.2 %all-gather = bf16[2048,128]{1,0:T(8,128)(2,1)} all-gather(bf16[128,128]{1,0:T(8,128)(2,1)S(1)} %convolution_convert_fusion.5), channel_id=2, replica_groups=mesh['ctx'=16,'exp'=32] {'ctx'}, dimensions={0}, use_global_device_ids=true | all-gather | bytes 557056 | tf_op jit(solution)/shard_map/all_gather | solution.py:14
  39.7 38.1 %all-reduce = bf16[16]{0:T(256)(128)(2,1)S(1)} all-reduce(bf16[16]{0:T(256)(128)(2,1)S(1)} %dynamic-update-slice), channel_id=1, replica_groups=mesh['ctx'=16,'exp'=32] {'ctx'}, use_global_device_ids=true, to_apply=%add | all-reduce | flops 16 | bytes 64
  78.9 1.3 fusion.2
  80.2 2.3 copy.121
  84.2 131.8 %reduce-scatter.10.cloned.1.call-done = bf16[96,128]{1,0:T(8,128)(2,1)} async-done(((bf16[3072,128]{1,0:T(8,128)(2,1)}), bf16[96,128]{1,0:T(8,128)(2,1)}) %reduce-scatter.10.cloned.1.call-update) | async-done | bytes 24592 | tf_op jit(solution)/shard_map/reduce_scatter | solution.py:96
  216.1 0.8 fusion.55
  216.8 45.9 %psum.14 = f32[128]{0:T(128)S(1)} all-reduce(f32[128]{0:T(128)S(1)} %get-tuple-element.215), channel_id=1, replica_groups=mesh['ctx'=16,'exp'=32] {'exp'}, use_global_device_ids=true, to_apply=%region_9.10 | all-reduce | flops 128 | bytes 1024 | tf_op jit(solution)/shard_map/psum | solution.py:109
  263.1 30.3 %all_to_all.66 = bf16[32,16,96]{2,1,0:T(8,128)(2,1)S(1)} all-to-all(bf16[32,16,96]{2,1,0:T(8,128)(2,1)S(1)} %bitcast.175), channel_id=1, replica_groups=mesh['ctx'=16,'exp'=32] {'exp'}, dimensions={0} | all-to-all | bytes 196608 | tf_op jit(solution)/shard_map/all_to_all | solution.py:126
  293.5 0.8 all_to_all.51
  295.0 20.5 %all_to_all.67 = bf16[32,16,96]{2,1,0:T(8,128)(2,1)S(1)} all-to-all(bf16[32,16,96]{2,1,0:T(8,128)(2,1)S(1)} %bitcast.176), channel_id=1, replica_groups=mesh['ctx'=16,'exp'=32] {'exp'}, dimensions={0} | all-to-all | bytes 196608 | tf_op jit(solution)/shard_map/all_to_all | solution.py:153
  315.5 0.8 all_to_all.58
  316.4 29.6 %all-gather.5.cloned.1.call-done = bf16[1,256,3072]{2,1,0:T(8,128)(2,1)} async-done(((bf16[1,16,3072]{2,1,0:T(8,128)(2,1)}), bf16[1,256,3072]{2,1,0:T(8,128)(2,1)}) %all-gather.5.cloned.1.call-update) | async-done | bytes 1572880 | tf_op jit(solution)/shard_map/all_gather | solution.py:127
  346.0 3.1 fusion.7
  349.1 59.1 %all-gather.7.cloned.1.call-done = bf16[1,256,3072]{2,1,0:T(8,128)(2,1)} async-done(((bf16[1,16,3072]{2,1,0:T(8,128)(2,1)}), bf16[1,256,3072]{2,1,0:T(8,128)(2,1)}) %all-gather.7.cloned.1.call-update) | async-done | bytes 1572880 | tf_op jit(solution)/shard_map/all_gather | solution.py:154
  408.2 5.2 fusion.1
  413.7 2.2 fusion
  415.9 86.2 %reduce-scatter.8.cloned.1.call-done = bf16[1,16,3072]{2,1,0:T(8,128)(2,1)} async-done(((bf16[1,256,3072]{2,1,0:T(8,128)(2,1)}), bf16[1,16,3072]{2,1,0:T(8,128)(2,1)}) %reduce-scatter.8.cloned.1.call-update) | async-done | bytes 98320 | tf_op jit(solution)/shard_map/reduce_scatter | solution.py:158
  502.1 3.6 copy.109
  506.2 18.0 %reduce.2 = bf16[3072,16]{1,0:T(8,128)(2,1)S(1)} reduce(bf16[3072,1,16]{2,1,0:T(2,128)(2,1)} %bitcast.168, bf16[]{:T(256)} %broadcast.70), dimensions={1}, to_apply=%bitcast.130.reduce_sub_computation | reduce | bytes 196610
  524.2 1.3 reshape.274
  525.5 12.9 %all-to-all-start.3 = ((bf16[32,2,768]{2,1,0:T(2,128)(2,1)}), bf16[32,2,768]{2,1,0:T(2,128)(2,1)}, u32[]{:S(2)}, u32[]{:S(2)}) async-start(bf16[32,2,768]{2,1,0:T(2,128)(2,1)} %reshape.274), calls=%async_computation.5 | async-start | bytes 196608 | tf_op jit(solution)/shard_map/all_to_all | solution.py:161
  538.3 56.6 %reduce-scatter.6.cloned.1.call-done = bf16[1,16,3072]{2,1,0:T(8,128)(2,1)} async-done(((bf16[1,256,3072]{2,1,0:T(8,128)(2,1)}), bf16[1,16,3072]{2,1,0:T(8,128)(2,1)}) %reduce-scatter.6.cloned.1.call-update) | async-done | bytes 98320 | tf_op jit(solution)/shard_map/reduce_scatter | solution.py:131
  595.0 3.6 copy.103
  598.6 18.0 %reduce.3 = bf16[3072,16]{1,0:T(8,128)(2,1)S(1)} reduce(bf16[3072,1,16]{2,1,0:T(2,128)(2,1)} %bitcast.169, bf16[]{:T(256)} %broadcast.70), dimensions={1}, to_apply=%bitcast.128.reduce_sub_computation | reduce | bytes 196610
  616.6 1.3 reshape.272
  617.9 12.8 %all-to-all-start.1 = ((bf16[32,2,768]{2,1,0:T(2,128)(2,1)}), bf16[32,2,768]{2,1,0:T(2,128)(2,1)S(1)}, u32[]{:S(2)}, u32[]{:S(2)}) async-start(bf16[32,2,768]{2,1,0:T(2,128)(2,1)} %reshape.272), calls=%async_computation.2 | async-start | bytes 196608 | tf_op jit(solution)/shard_map/all_to_all | solution.py:134
  630.7 4.9 reshape.275
  635.6 3.3 copy.110
  639.4 45.4 %psum.15 = f32[128]{0:T(128)S(1)} all-reduce(f32[128]{0:T(128)S(1)} %get-tuple-element.221), channel_id=1, replica_groups=mesh['ctx'=16,'exp'=32] {'exp'}, use_global_device_ids=true, to_apply=%region_14.15 | all-reduce | flops 128 | bytes 1024 | tf_op jit(solution)/shard_map/psum | solution.py:165
  685.3 2.4 reshape.273
  687.8 3.4 copy.104
  691.5 1.0 fusion.22
  692.5 1.4 fusion.61
  693.9 33.0 %all_gather.32 = bf16[128,3072]{0,1:T(8,128)(2,1)S(1)} all-gather(bf16[128,96]{0,1:T(8,128)(2,1)S(1)} %get-tuple-element.217), channel_id=1, replica_groups=mesh['ctx'=16,'exp'=32] {'exp'}, dimensions={1}, use_global_device_ids=true | all-gather | bytes 811008 | tf_op jit(solution)/shard_map/all_gather | solution.py:172
  728.6 23.3 %all-gather.1 = bf16[2048,128]{1,0:T(8,128)(2,1)S(1)} all-gather(bf16[128,128]{1,0:T(8,128)(2,1)S(1)} %convolution_convert_fusion.4), channel_id=3, replica_groups=mesh['ctx'=16,'exp'=32] {'ctx'}, dimensions={0}, use_global_device_ids=true | all-gather | bytes 557056 | tf_op jit(solution)/shard_map/all_gather | solution.py:14
  751.9 19.2 %while.27 = (s32[]{:T(128)}, f32[1,128,128]{2,1,0:T(8,128)S(1)}, s32[]{:T(128)}, bf16[16,1,128,128]{3,2,1,0:T(8,128)(2,1)S(1)}, bf16[16,1]{0,1:T(2,128)(2,1)S(1)...) while((s32[]{:T(128)}, f32[1,128,128]{2,1,0:T(8,128)S(1)}, s32[]{:T(128)}, ...), condition=%wide.region_16.17_spmd, body=%wide.region_15.16_spmd.sunk | while | flops 49158 | bytes 163997 | solution.py:29
  752.5 0.7 convert_add_fusion.6
  753.8 0.7 convert_add_fusion.6
  755.1 0.7 convert_add_fusion.6
  756.4 0.7 convert_add_fusion.6
  757.7 0.7 convert_add_fusion.6
  771.2 0.8 fusion.33
  772.0 0.8 fusion.32
  772.8 0.9 fusion.31
  (130 shorter events, 24.2 us)
Async XLA Ops:
  7.2 401.1 %copy-start = (bf16[1,384,3072]{2,1,0:T(8,128)(2,1)S(1)}, bf16[1,384,3072]{2,1,0:T(8,128)(2,1)}, u32[]{:S(2)}) copy-start(bf16[1,384,3072]{2,1,0:T(8,128)(2,1)} %param.22) | copy-start | bytes 7077892
  7.2 70.7 %copy-start.5 = (bf16[128,128]{1,0:T(8,128)(2,1)S(1)}, bf16[128,128]{1,0:T(8,128)(2,1)}, u32[]{:S(2)}) copy-start(bf16[128,128]{1,0:T(8,128)(2,1)} %param.17) | copy-start | bytes 98308
  7.2 70.9 %copy-start.3 = (bf16[128,128]{1,0:T(8,128)(2,1)S(1)}, bf16[128,128]{1,0:T(8,128)(2,1)}, u32[]{:S(2)}) copy-start(bf16[128,128]{1,0:T(8,128)(2,1)} %param.18) | copy-start | bytes 98308
  7.2 70.7 %copy-start.7 = (bf16[128,128]{1,0:T(8,128)(2,1)S(1)}, bf16[128,128]{1,0:T(8,128)(2,1)}, u32[]{:S(2)}) copy-start(bf16[128,128]{1,0:T(8,128)(2,1)} %param.16) | copy-start | bytes 98308
  7.2 71.6 %copy-start.1 = (bf16[128,3072]{1,0:T(8,128)(2,1)S(1)}, bf16[128,3072]{1,0:T(8,128)(2,1)}, u32[]{:S(2)}) copy-start(bf16[128,3072]{1,0:T(8,128)(2,1)} %param.20) | copy-start | bytes 2359300
  7.2 208.8 %reduce-scatter.10.cloned.1.call-start = ((), (), s32[]{:S(2)}) async-start(), calls=%async_computation.11 | async-start | bytes 811008 | tf_op jit(solution)/shard_map/reduce_scatter | solution.py:96
  8.4 71.8 %copy-start.18 = (f32[1,128]{1,0:T(1,128)}, f32[1,128]{1,0:T(1,128)S(1)}, u32[]{:S(2)}) copy-start(f32[1,128]{1,0:T(1,128)S(1)} %reduce_window_sum.26) | copy-start | bytes 1540
  10.3 67.5 %copy-start.16 = (f32[128]{0:T(128)}, f32[128]{0:T(128)S(1)}, u32[]{:S(2)}) copy-start(f32[128]{0:T(128)S(1)} %get-tuple-element.220) | copy-start | bytes 1540
  10.3 69.8 %copy-start.14 = (f32[128]{0:T(128)}, f32[128]{0:T(128)S(1)}, u32[]{:S(2)}) copy-start(f32[128]{0:T(128)S(1)} %get-tuple-element.219) | copy-start | bytes 1540
  77.9 4.6 copy-start.23
  78.1 0.6 copy-start.9
  80.1 2.4 copy-start.20
  80.1 135.9 %copy-start.13 = (bf16[128,96]{0,1:T(8,128)(2,1)S(1)}, bf16[128,96]{0,1:T(8,128)(2,1)}, u32[]{:S(2)}) copy-start(bf16[128,96]{0,1:T(8,128)(2,1)} %param.15) | copy-start | bytes 73732
  82.5 211.9 %copy-start.22 = (f32[128,2]{0,1:T(2,128)S(1)}, f32[128,2]{0,1:T(2,128)}, u32[]{:S(2)}) copy-start(f32[128,2]{0,1:T(2,128)} %param.24) | copy-start | bytes 3076
  82.5 212.2 %copy-start.12 = (bf16[128,96]{0,1:T(8,128)(2,1)S(1)}, bf16[128,96]{0,1:T(8,128)(2,1)}, u32[]{:S(2)}) copy-start(bf16[128,96]{0,1:T(8,128)(2,1)} %param.25) | copy-start | bytes 73732
  82.5 263.5 %all-gather.5.cloned.1.call-start = ((), (), s32[]{:S(2)}) async-start(), calls=%async_computation.7 | async-start | bytes 1671168 | tf_op jit(solution)/shard_map/all_gather | solution.py:127
  262.8 31.6 %copy-start.21 = (f32[128]{0:T(128)}, f32[128]{0:T(128)S(1)}, u32[]{:S(2)}) copy-start(f32[128]{0:T(128)S(1)} %add_rsqrt_fusion) | copy-start | bytes 1540
  294.3 113.9 %all-gather.7.cloned.1.call-start = ((), (), s32[]{:S(2)}) async-start(), calls=%async_computation.9 | async-start | bytes 1671168 | tf_op jit(solution)/shard_map/all_gather | solution.py:154
  316.4 185.7 %reduce-scatter.8.cloned.1.call-start = ((), (), s32[]{:S(2)}) async-start(), calls=%async_computation.10 | async-start | bytes 1671168 | tf_op jit(solution)/shard_map/reduce_scatter | solution.py:158
  413.5 181.5 %reduce-scatter.6.cloned.1.call-start = ((), (), s32[]{:S(2)}) async-start(), calls=%async_computation.8 | async-start | bytes 1671168 | tf_op jit(solution)/shard_map/reduce_scatter | solution.py:131
  525.5 92.4 %all-to-all-start.3 = ((bf16[32,2,768]{2,1,0:T(2,128)(2,1)}), bf16[32,2,768]{2,1,0:T(2,128)(2,1)}, u32[]{:S(2)}, u32[]{:S(2)}) async-start(bf16[32,2,768]{2,1,0:T(2,128)(2,1)} %reshape.274), calls=%async_computation.5 | async-start | bytes 196608 | tf_op jit(solution)/shard_map/all_to_all | solution.py:161
  617.9 67.5 %all-to-all-start.1 = ((bf16[32,2,768]{2,1,0:T(2,128)(2,1)}), bf16[32,2,768]{2,1,0:T(2,128)(2,1)S(1)}, u32[]{:S(2)}, u32[]{:S(2)}) async-start(bf16[32,2,768]{2,1,0:T(2,128)(2,1)} %reshape.272), calls=%async_computation.2 | async-start | bytes 196608 | tf_op jit(solution)/shard_map/all_to_all | solution.py:134
  687.7 39.1 %copy-start.2 = (bf16[128,3072]{1,0:T(8,128)(2,1)S(1)}, bf16[128,3072]{1,0:T(8,128)(2,1)}, u32[]{:S(2)}) copy-start(bf16[128,3072]{1,0:T(8,128)(2,1)} %param.20) | copy-start | bytes 2359300
  691.3 35.9 %copy-start.8 = (bf16[128,128]{1,0:T(8,128)(2,1)S(1)}, bf16[128,128]{1,0:T(8,128)(2,1)}, u32[]{:S(2)}) copy-start(bf16[128,128]{1,0:T(8,128)(2,1)} %param.16) | copy-start | bytes 98308
  691.4 35.9 %copy-start.15 = (f32[128]{0:T(128)S(1)}, f32[128]{0:T(128)}, u32[]{:S(2)}) copy-start(f32[128]{0:T(128)} %copy-done.14) | copy-start | bytes 1540
  691.4 36.2 %copy-start.10 = (f32[128,128]{1,0:T(8,128)S(1)}, f32[128,128]{1,0:T(8,128)}, u32[]{:S(2)}) copy-start(f32[128,128]{1,0:T(8,128)} %copy-done.9) | copy-start | bytes 196612
  691.4 36.5 %copy-start.4 = (bf16[128,128]{1,0:T(8,128)(2,1)S(1)}, bf16[128,128]{1,0:T(8,128)(2,1)}, u32[]{:S(2)}) copy-start(bf16[128,128]{1,0:T(8,128)(2,1)} %param.18) | copy-start | bytes 98308
  691.4 36.5 %copy-start.19 = (f32[1,128]{1,0:T(1,128)S(1)}, f32[1,128]{1,0:T(1,128)}, u32[]{:S(2)}) copy-start(f32[1,128]{1,0:T(1,128)} %copy-done.18) | copy-start | bytes 1540
  693.9 34.8 %copy-start.11 = (bf16[128,96]{0,1:T(8,128)(2,1)}, bf16[128,96]{0,1:T(8,128)(2,1)S(1)}, u32[]{:S(2)}) copy-start(bf16[128,96]{0,1:T(8,128)(2,1)S(1)} %get-tuple-element.217) | copy-start | bytes 73732
  693.9 34.6 %copy-start.6 = (bf16[128,128]{1,0:T(8,128)(2,1)S(1)}, bf16[128,128]{1,0:T(8,128)(2,1)}, u32[]{:S(2)}) copy-start(bf16[128,128]{1,0:T(8,128)(2,1)} %param.17) | copy-start | bytes 98308
  726.9 25.1 %copy-start.24 = (bf16[16,1]{0,1:T(2,128)(2,1)S(1)}, bf16[16,1]{0,1:T(2,128)(2,1)}, u32[]{:S(2)}) copy-start(bf16[16,1]{0,1:T(2,128)(2,1)} %copy-done.23) | copy-start | bytes 100
  727.3 43.9 %copy-start.17 = (f32[128]{0:T(128)S(1)}, f32[128]{0:T(128)}, u32[]{:S(2)}) copy-start(f32[128]{0:T(128)} %copy-done.16) | copy-start | bytes 1540
Sparse Core Ops, SparseCore 0:
  82.6 133.4 reduce-scatter.9
  294.4 51.4 all-gather.4
  349.5 58.7 all-gather.6
  413.6 88.4 reduce-scatter.7
  506.6 88.3 reduce-scatter.5
where the time goes:
time: 783 us; the launch traced here: 780 us
  waiting for transfers between devices  363 us (46%)
  blocking collectives  263 us (34%)
  other arithmetic  51.2 us (7%)
  local copies, waits for them, and re-layouts  41.8 us (5%)
  starting transfers between devices  26.1 us (3%)
  matrix products  19.5 us (2%)
  between operations  15 us (2%)
    reduce_scatter x1, waiting for transfers between devices, local(): lax.psum_scatter(lax.dot_general(columns, attn_heads, (((0,), (1,)), ((),...  132 us
    reduce_scatter x1, waiting for transfers between devices, local(): lax.psum_scatter(partial_grad.astype(jnp.bfloat16), 'ctx', scatter_dimens...  86.2 us
    all_gather x1, waiting for transfers between devices, local(): grad_all = lax.all_gather(grad_in, 'ctx', axis=1, tiled=True)  59.1 us
    reduce_scatter x1, waiting for transfers between devices, local(): lax.psum_scatter(partial_out.astype(jnp.bfloat16), 'ctx', scatter_dimensi...  56.6 us
    all_gather x2, blocking collectives, prefix(): lax.all_gather(a.astype(kind), axis)  49.5 us
    psum x1, blocking collectives, local(): square_sum = lax.psum(jnp.sum(residual_f * residual_f, axis=1), 'exp')  45.9 us
    psum x1, blocking collectives, local(): inner_dot = lax.psum(jnp.sum(grad_normed * residual_f, axis=1), 'exp')  45.4 us
    unnamed x1, blocking collectives  38.1 us
  transfers between devices with their start and end apart: 7, of which 5 were waited for; matrix products, arithmetic and copies ran while one was open for 8% of the time, Pallas kernels for 0%

commit v1 on v0

--- a/solution.py
+++ b/solution.py
@@ -151,7 +151,9 @@
         .reshape(expert_count, capacity, share)
     )
     grad_in = lax.all_to_all(grad_send, "exp", split_axis=0, concat_axis=2, tiled=True)
-    grad_all = lax.all_gather(grad_in, "ctx", axis=1, tiled=True)
+    grad_all = jnp.concatenate(
+        lax.all_to_all(jnp.stack([grad_in] * lax.axis_size("ctx")), "ctx", 0, 0), axis=1
+    )
     grad_act = jnp.einsum("erd,efd->erf", grad_all, w_down, preferred_element_type=jnp.float32)
     grad_up = (grad_act * silu_grad(upper)).astype(jnp.bfloat16)
     partial_grad = jnp.einsum("erf,edf->erd", grad_up, w_up, preferred_element_type=jnp.float32)

time: 783 us -> 731 us (0.934)
  waiting for transfers between devices: 363 us -> 302 us
    all_gather x1 -> x0, waiting for transfers between devices: 59.1 us -> none  [local(): grad_all = lax.all_gather(grad_in, 'ctx', axis=1, tiled=True)]
  transfers between devices with their start and end apart: 7 -> 7, of which waited for: 5 -> 4; matrix products, arithmetic and copies ran while one was open for 8% -> 9% of each run, Pallas kernels for 0% -> 0%
where the time goes in v1:
time: 731 us; the launch traced here: 728 us
  waiting for transfers between devices  302 us (41%)
  blocking collectives  262 us (36%)
  other arithmetic  51.2 us (7%)
  local copies, waits for them, and re-layouts  42.6 us (6%)
  starting transfers between devices  33.3 us (5%)
  matrix products  20.9 us (3%)
  between operations  14.9 us (2%)
    reduce_scatter x1, waiting for transfers between devices, local(): lax.psum_scatter(lax.dot_general(columns, attn_heads, (((0,), (1,)), ((),...  135 us
    reduce_scatter x1, waiting for transfers between devices, local(): lax.psum_scatter(partial_grad.astype(jnp.bfloat16), 'ctx', scatter_dimens...  82.1 us
    reduce_scatter x1, waiting for transfers between devices, local(): lax.psum_scatter(partial_out.astype(jnp.bfloat16), 'ctx', scatter_dimensi...  56.7 us
    all_gather x2, blocking collectives, prefix(): lax.all_gather(a.astype(kind), axis)  46.7 us
    psum x1, blocking collectives, local(): square_sum = lax.psum(jnp.sum(residual_f * residual_f, axis=1), 'exp')  46 us
    psum x1, blocking collectives, local(): inner_dot = lax.psum(jnp.sum(grad_normed * residual_f, axis=1), 'exp')  45.4 us
    unnamed x1, blocking collectives  40.7 us
    unnamed x2, other arithmetic  36 us
  transfers between devices with their start and end apart: 7, of which 4 were waited for; matrix products, arithmetic and copies ran while one was open for 9% of the time, Pallas kernels for 0%

profile of v1, /device:TPU:32, one launch (start us, length us, event | category | flops | bytes accessed | tf_op | source)
XLA Modules:
  0.0 727.6 jit_solution(4353793323779455137)
XLA Ops:
  7.3 1.1 reduce_window_sum.26
  9.6 1.3 dynamic-slice
  10.9 0.8 dynamic-update-slice
  11.6 40.7 %all-reduce = bf16[16]{0:T(256)(128)(2,1)S(1)} all-reduce(bf16[16]{0:T(256)(128)(2,1)S(1)} %dynamic-update-slice), channel_id=1, replica_groups=mesh['ctx'=16,'exp'=32] {'ctx'}, use_global_device_ids=true, to_apply=%add | all-reduce | flops 16 | bytes 64
  53.0 0.9 convolution_multiply_fusion.7
  53.9 1.0 fusion.75
  54.9 1.1 convolution_convert_fusion.5
  56.0 23.5 %all-gather = bf16[2048,128]{1,0:T(8,128)(2,1)} all-gather(bf16[128,128]{1,0:T(8,128)(2,1)S(1)} %convolution_convert_fusion.5), channel_id=2, replica_groups=mesh['ctx'=16,'exp'=32] {'ctx'}, dimensions={0}, use_global_device_ids=true | all-gather | bytes 557056 | tf_op jit(solution)/shard_map/all_gather | solution.py:14
  79.7 1.3 fusion.2
  81.0 2.3 copy.121
  85.1 135.1 %reduce-scatter.10.cloned.1.call-done = bf16[96,128]{1,0:T(8,128)(2,1)} async-done(((bf16[3072,128]{1,0:T(8,128)(2,1)}), bf16[96,128]{1,0:T(8,128)(2,1)}) %reduce-scatter.10.cloned.1.call-update) | async-done | bytes 24592 | tf_op jit(solution)/shard_map/reduce_scatter | solution.py:96
  220.2 0.8 fusion.48
  221.0 46.0 %psum.14 = f32[128]{0:T(128)S(1)} all-reduce(f32[128]{0:T(128)S(1)} %get-tuple-element.215), channel_id=1, replica_groups=mesh['ctx'=16,'exp'=32] {'exp'}, use_global_device_ids=true, to_apply=%region_9.10 | all-reduce | flops 128 | bytes 1024 | tf_op jit(solution)/shard_map/psum | solution.py:109
  267.8 29.9 %all_to_all.68 = bf16[32,16,96]{2,1,0:T(8,128)(2,1)S(1)} all-to-all(bf16[32,16,96]{2,1,0:T(8,128)(2,1)S(1)} %bitcast.168), channel_id=1, replica_groups=mesh['ctx'=16,'exp'=32] {'exp'}, dimensions={0} | all-to-all | bytes 196608 | tf_op jit(solution)/shard_map/all_to_all | solution.py:126
  297.7 0.8 all_to_all.52
  299.2 20.5 %all_to_all.69 = bf16[32,16,96]{2,1,0:T(8,128)(2,1)S(1)} all-to-all(bf16[32,16,96]{2,1,0:T(8,128)(2,1)S(1)} %bitcast.169), channel_id=1, replica_groups=mesh['ctx'=16,'exp'=32] {'exp'}, dimensions={0} | all-to-all | bytes 196608 | tf_op jit(solution)/shard_map/all_to_all | solution.py:153
  319.9 1.3 stack.5
  321.2 7.3 %all-to-all-start.3 = ((bf16[16,1,16,3072]{3,2,1,0:T(8,128)(2,1)}), bf16[16,1,16,3072]{3,2,1,0:T(8,128)(2,1)}, u32[]{:S(2)}, u32[]{:S(2)}) async-start(bf16[16,1,16,3072]{3,2,1,0:T(8,128)(2,1)} %stack.5), calls=%async_computation.4 | async-start | bytes 3145728 | tf_op jit(solution)/shard_map/all_to_all | solution.py:155
  328.5 28.1 %all-gather.4.cloned.1.call-done = bf16[1,256,3072]{2,1,0:T(8,128)(2,1)} async-done(((bf16[1,16,3072]{2,1,0:T(8,128)(2,1)}), bf16[1,256,3072]{2,1,0:T(8,128)(2,1)}) %all-gather.4.cloned.1.call-update) | async-done | bytes 1572880 | tf_op jit(solution)/shard_map/all_gather | solution.py:127
  356.6 3.1 fusion.7
  359.8 5.2 fusion.1
  365.3 2.2 fusion
  367.4 82.1 %reduce-scatter.8.cloned.1.call-done = bf16[1,16,3072]{2,1,0:T(8,128)(2,1)} async-done(((bf16[1,256,3072]{2,1,0:T(8,128)(2,1)}), bf16[1,16,3072]{2,1,0:T(8,128)(2,1)}) %reduce-scatter.8.cloned.1.call-update) | async-done | bytes 98320 | tf_op jit(solution)/shard_map/reduce_scatter | solution.py:160
  449.5 3.6 copy.109
  453.6 18.0 %reduce.2 = bf16[3072,16]{1,0:T(8,128)(2,1)S(1)} reduce(bf16[3072,1,16]{2,1,0:T(2,128)(2,1)} %bitcast.161, bf16[]{:T(256)} %broadcast.72), dimensions={1}, to_apply=%bitcast.122.reduce_sub_computation | reduce | bytes 196610
  471.6 1.3 reshape.281
  472.9 12.9 %all-to-all-start.4 = ((bf16[32,2,768]{2,1,0:T(2,128)(2,1)}), bf16[32,2,768]{2,1,0:T(2,128)(2,1)}, u32[]{:S(2)}, u32[]{:S(2)}) async-start(bf16[32,2,768]{2,1,0:T(2,128)(2,1)} %reshape.281), calls=%async_computation.6 | async-start | bytes 196608 | tf_op jit(solution)/shard_map/all_to_all | solution.py:163
  485.8 56.7 %reduce-scatter.6.cloned.1.call-done = bf16[1,16,3072]{2,1,0:T(8,128)(2,1)} async-done(((bf16[1,256,3072]{2,1,0:T(8,128)(2,1)}), bf16[1,16,3072]{2,1,0:T(8,128)(2,1)}) %reduce-scatter.6.cloned.1.call-update) | async-done | bytes 98320 | tf_op jit(solution)/shard_map/reduce_scatter | solution.py:131
  542.5 3.6 copy.103
  546.1 18.0 %reduce.3 = bf16[3072,16]{1,0:T(8,128)(2,1)S(1)} reduce(bf16[3072,1,16]{2,1,0:T(2,128)(2,1)} %bitcast.162, bf16[]{:T(256)} %broadcast.72), dimensions={1}, to_apply=%bitcast.120.reduce_sub_computation | reduce | bytes 196610
  564.1 1.3 reshape.279
  565.4 12.8 %all-to-all-start.1 = ((bf16[32,2,768]{2,1,0:T(2,128)(2,1)}), bf16[32,2,768]{2,1,0:T(2,128)(2,1)S(1)}, u32[]{:S(2)}, u32[]{:S(2)}) async-start(bf16[32,2,768]{2,1,0:T(2,128)(2,1)} %reshape.279), calls=%async_computation.2 | async-start | bytes 196608 | tf_op jit(solution)/shard_map/all_to_all | solution.py:134
  578.2 4.9 reshape.282
  583.1 3.3 copy.110
  586.7 0.8 fusion.51
  587.5 45.4 %psum.15 = f32[128]{0:T(128)S(1)} all-reduce(f32[128]{0:T(128)S(1)} %get-tuple-element.221), channel_id=1, replica_groups=mesh['ctx'=16,'exp'=32] {'exp'}, use_global_device_ids=true, to_apply=%region_14.15 | all-reduce | flops 128 | bytes 1024 | tf_op jit(solution)/shard_map/psum | solution.py:167
  633.4 2.4 reshape.280
  635.8 3.4 copy.104
  639.8 1.4 fusion.54
  641.3 33.0 %all_gather.28 = bf16[128,3072]{0,1:T(8,128)(2,1)S(1)} all-gather(bf16[128,96]{0,1:T(8,128)(2,1)S(1)} %get-tuple-element.217), channel_id=1, replica_groups=mesh['ctx'=16,'exp'=32] {'exp'}, dimensions={1}, use_global_device_ids=true | all-gather | bytes 811008 | tf_op jit(solution)/shard_map/all_gather | solution.py:174
  676.1 0.9 fusion.26
  677.0 23.2 %all-gather.1 = bf16[2048,128]{1,0:T(8,128)(2,1)S(1)} all-gather(bf16[128,128]{1,0:T(8,128)(2,1)S(1)} %convolution_convert_fusion.4), channel_id=3, replica_groups=mesh['ctx'=16,'exp'=32] {'ctx'}, dimensions={0}, use_global_device_ids=true | all-gather | bytes 557056 | tf_op jit(solution)/shard_map/all_gather | solution.py:14
  700.2 19.2 %while.27 = (s32[]{:T(128)}, f32[1,128,128]{2,1,0:T(8,128)S(1)}, s32[]{:T(128)}, bf16[16,1,128,128]{3,2,1,0:T(8,128)(2,1)S(1)}, bf16[16,1]{0,1:T(2,128)(2,1)S(1)...) while((s32[]{:T(128)}, f32[1,128,128]{2,1,0:T(8,128)S(1)}, s32[]{:T(128)}, ...), condition=%wide.region_16.17_spmd, body=%wide.region_15.16_spmd.sunk | while | flops 49158 | bytes 164005 | solution.py:29
  700.9 0.7 convert_add_fusion.6
  702.1 0.7 convert_add_fusion.6
  703.4 0.7 convert_add_fusion.6
  719.4 0.8 fusion.27
  720.2 0.8 fusion.28
  (124 shorter events, 25.5 us)
Async XLA Ops:
  7.2 352.6 %copy-start = (bf16[1,384,3072]{2,1,0:T(8,128)(2,1)S(1)}, bf16[1,384,3072]{2,1,0:T(8,128)(2,1)}, u32[]{:S(2)}) copy-start(bf16[1,384,3072]{2,1,0:T(8,128)(2,1)} %param.22) | copy-start | bytes 7077892
  7.2 72.3 %copy-start.5 = (bf16[128,128]{1,0:T(8,128)(2,1)S(1)}, bf16[128,128]{1,0:T(8,128)(2,1)}, u32[]{:S(2)}) copy-start(bf16[128,128]{1,0:T(8,128)(2,1)} %param.16) | copy-start | bytes 98308
  7.2 72.5 %copy-start.1 = (bf16[128,3072]{1,0:T(8,128)(2,1)S(1)}, bf16[128,3072]{1,0:T(8,128)(2,1)}, u32[]{:S(2)}) copy-start(bf16[128,3072]{1,0:T(8,128)(2,1)} %param.20) | copy-start | bytes 2359300
  7.2 213.0 %reduce-scatter.10.cloned.1.call-start = ((), (), s32[]{:S(2)}) async-start(), calls=%async_computation.11 | async-start | bytes 811008 | tf_op jit(solution)/shard_map/reduce_scatter | solution.py:96
  8.4 71.1 %copy-start.15 = (f32[1,128]{1,0:T(1,128)}, f32[1,128]{1,0:T(1,128)S(1)}, u32[]{:S(2)}) copy-start(f32[1,128]{1,0:T(1,128)S(1)} %reduce_window_sum.26) | copy-start | bytes 1540
  53.0 28.0 %copy-start.11 = (f32[128]{0:T(128)}, f32[128]{0:T(128)S(1)}, u32[]{:S(2)}) copy-start(f32[128]{0:T(128)S(1)} %get-tuple-element.220) | copy-start | bytes 1540
  53.0 28.0 %copy-start.13 = (f32[128]{0:T(128)}, f32[128]{0:T(128)S(1)}, u32[]{:S(2)}) copy-start(f32[128]{0:T(128)S(1)} %get-tuple-element.219) | copy-start | bytes 1540
  53.9 27.1 %copy-start.6 = (f32[128,128]{1,0:T(8,128)}, f32[128,128]{1,0:T(8,128)S(1)}, u32[]{:S(2)}) copy-start(f32[128,128]{1,0:T(8,128)S(1)} %convolution_multiply_fusion.7) | copy-start | bytes 196612
  79.5 3.8 copy-start.20
  81.0 2.4 copy-start.17
  81.0 139.2 %copy-start.10 = (bf16[128,96]{0,1:T(8,128)(2,1)S(1)}, bf16[128,96]{0,1:T(8,128)(2,1)}, u32[]{:S(2)}) copy-start(bf16[128,96]{0,1:T(8,128)(2,1)} %param.15) | copy-start | bytes 73732
  83.3 215.2 %copy-start.19 = (f32[128,2]{0,1:T(2,128)S(1)}, f32[128,2]{0,1:T(2,128)}, u32[]{:S(2)}) copy-start(f32[128,2]{0,1:T(2,128)} %param.24) | copy-start | bytes 3076
  83.3 215.5 %copy-start.9 = (bf16[128,96]{0,1:T(8,128)(2,1)S(1)}, bf16[128,96]{0,1:T(8,128)(2,1)}, u32[]{:S(2)}) copy-start(bf16[128,96]{0,1:T(8,128)(2,1)} %param.25) | copy-start | bytes 73732
  83.4 273.3 %all-gather.4.cloned.1.call-start = ((), (), s32[]{:S(2)}) async-start(), calls=%async_computation.8 | async-start | bytes 1671168 | tf_op jit(solution)/shard_map/all_gather | solution.py:127
  266.9 0.5 copy-start.18
  321.2 38.6 %all-to-all-start.3 = ((bf16[16,1,16,3072]{3,2,1,0:T(8,128)(2,1)}), bf16[16,1,16,3072]{3,2,1,0:T(8,128)(2,1)}, u32[]{:S(2)}, u32[]{:S(2)}) async-start(bf16[16,1,16,3072]{3,2,1,0:T(8,128)(2,1)} %stack.5), calls=%async_computation.4 | async-start | bytes 3145728 | tf_op jit(solution)/shard_map/all_to_all | solution.py:155
  328.5 121.1 %reduce-scatter.8.cloned.1.call-start = ((), (), s32[]{:S(2)}) async-start(), calls=%async_computation.10 | async-start | bytes 1671168 | tf_op jit(solution)/shard_map/reduce_scatter | solution.py:160
  365.0 177.5 %reduce-scatter.6.cloned.1.call-start = ((), (), s32[]{:S(2)}) async-start(), calls=%async_computation.9 | async-start | bytes 1671168 | tf_op jit(solution)/shard_map/reduce_scatter | solution.py:131
  472.9 92.5 %all-to-all-start.4 = ((bf16[32,2,768]{2,1,0:T(2,128)(2,1)}), bf16[32,2,768]{2,1,0:T(2,128)(2,1)}, u32[]{:S(2)}, u32[]{:S(2)}) async-start(bf16[32,2,768]{2,1,0:T(2,128)(2,1)} %reshape.281), calls=%async_computation.6 | async-start | bytes 196608 | tf_op jit(solution)/shard_map/all_to_all | solution.py:163
  565.4 68.0 %all-to-all-start.1 = ((bf16[32,2,768]{2,1,0:T(2,128)(2,1)}), bf16[32,2,768]{2,1,0:T(2,128)(2,1)S(1)}, u32[]{:S(2)}, u32[]{:S(2)}) async-start(bf16[32,2,768]{2,1,0:T(2,128)(2,1)} %reshape.279), calls=%async_computation.2 | async-start | bytes 196608 | tf_op jit(solution)/shard_map/all_to_all | solution.py:134
  635.8 38.5 %copy-start.2 = (bf16[128,3072]{1,0:T(8,128)(2,1)S(1)}, bf16[128,3072]{1,0:T(8,128)(2,1)}, u32[]{:S(2)}) copy-start(bf16[128,3072]{1,0:T(8,128)(2,1)} %param.20) | copy-start | bytes 2359300
  639.4 35.3 %copy-start.3 = (bf16[128,128]{1,0:T(8,128)(2,1)S(1)}, bf16[128,128]{1,0:T(8,128)(2,1)}, u32[]{:S(2)}) copy-start(bf16[128,128]{1,0:T(8,128)(2,1)} %param.18) | copy-start | bytes 98308
  639.4 35.3 %copy-start.16 = (f32[1,128]{1,0:T(1,128)S(1)}, f32[1,128]{1,0:T(1,128)}, u32[]{:S(2)}) copy-start(f32[1,128]{1,0:T(1,128)} %copy-done.15) | copy-start | bytes 1540
  639.5 35.4 %copy-start.4 = (bf16[128,128]{1,0:T(8,128)(2,1)S(1)}, bf16[128,128]{1,0:T(8,128)(2,1)}, u32[]{:S(2)}) copy-start(bf16[128,128]{1,0:T(8,128)(2,1)} %param.17) | copy-start | bytes 98308
  639.8 35.6 %copy-start.14 = (f32[128]{0:T(128)S(1)}, f32[128]{0:T(128)}, u32[]{:S(2)}) copy-start(f32[128]{0:T(128)} %copy-done.13) | copy-start | bytes 1540
  641.3 34.8 %copy-start.8 = (bf16[128,96]{0,1:T(8,128)(2,1)}, bf16[128,96]{0,1:T(8,128)(2,1)S(1)}, u32[]{:S(2)}) copy-start(bf16[128,96]{0,1:T(8,128)(2,1)S(1)} %get-tuple-element.217) | copy-start | bytes 73732
  641.3 34.5 %copy-start.7 = (f32[128,128]{1,0:T(8,128)S(1)}, f32[128,128]{1,0:T(8,128)}, u32[]{:S(2)}) copy-start(f32[128,128]{1,0:T(8,128)} %copy-done.6) | copy-start | bytes 196612
  674.3 25.9 %copy-start.21 = (bf16[16,1]{0,1:T(2,128)(2,1)S(1)}, bf16[16,1]{0,1:T(2,128)(2,1)}, u32[]{:S(2)}) copy-start(bf16[16,1]{0,1:T(2,128)(2,1)} %copy-done.20) | copy-start | bytes 100
  674.7 44.7 %copy-start.12 = (f32[128]{0:T(128)S(1)}, f32[128]{0:T(128)}, u32[]{:S(2)}) copy-start(f32[128]{0:T(128)} %copy-done.11) | copy-start | bytes 1540
Sparse Core Ops, SparseCore 0:
  83.5 136.6 reduce-scatter.9
  298.6 57.9 all-gather.3
  365.1 84.3 reduce-scatter.7
  454.0 88.4 reduce-scatter.5
